TPU v7x, 32 devices: a whole 2x2x4 slice. The times are simulated.
32 devices in a mesh: grp: 2 (over y), pix: 4 (over z), chan: 2 (over x), sub: 2 (over core).
Axes of the slice: x: 2, y: 2, z: 4, core: 2. Of those that a mesh axis runs over, the one named last changes fastest.
Arguments:
- features: bfloat16 [256, 131072], P('chan', ('grp', 'pix', 'sub')), parts along dimension 1, may hold values from -6 to 6
- neighbours: int32 [8, 131072], P(None, ('grp', 'pix', 'sub')), parts along dimension 1, may hold values from 0 to 8703, as said below
- live_cols: int32 [16], P(('grp', 'pix', 'sub')), parts along dimension 0, may hold values from 8 to 32, as said below
- cheb_weight: bfloat16 [7, 256, 256], replicated, may hold values from -0.125 to 0.125
- out_bias: float32 [256], replicated, may hold values from -3 to 3
Outputs:
- mixed: bfloat16 [16, 8192, 256], P(('grp', 'pix', 'sub'), 'chan'), parts along dimension 0
There are 2 independent parts, one for each index of `grp`. A program takes and returns all parts, laid end to end along the dimension named above; an argument that names none is the same for every part. Nothing has to cross between parts.
Inputs may be any that keep to these rules, and one draw needn't show every extreme that they name: `live_cols`: every patch has at least 8 live columns; some patch has all 32 columns live. `neighbours`: Entry t of a live slot at column c and latitude l names either the slot itself (extended index 256 + s) or the slot at column c + dc and latitude l + dl, with (dc, dl) = (-1,-1), (-1,0), (-1,1), (0,-1), (0,1), (1,-1), (1,0), (1,1) for t = 0 to 7; column -1 means the last live column of the previous patch and column live_cols[p] the first column of the next patch, and the latitude stays within 0 to 255. Dead slots name only themselves.
All inputs are finite; a program needn't handle non-finite values.
Results may differ from a plain program's by a relative error of at most 0.0039.
Values may be sent and summed in bfloat16 or wider, within the bound.
No kernel may reach another device: no remote copies, remote signals or barrier semaphores. Data moves between devices by JAX's collectives and lax.ppermute only.
A program may use at most 64 MiB of HBM per device.

v0:
```python
import jax
import jax.numpy as jnp
from jax import lax
from jax.sharding import PartitionSpec as P

DEG = 6
LATS = 256
tap_offsets = [(-1, -1), (-1, 0), (-1, 1), (0, -1), (0, 1), (1, -1), (1, 0), (1, 1)]


def shifted(value, axis, steps):
    count = lax.axis_size(axis)
    pairs = [(source, (source + steps) % count) for source in range(count)]
    return lax.ppermute(value, axis, pairs)


def tap_sum(padded, present, start, width):
    center = lax.slice_in_dim(padded, start, start + width, axis=1)
    summed = jnp.zeros(center.shape, jnp.float32)
    for tap_index in range(8):
        step_col, step_lat = tap_offsets[tap_index]
        moved_start = start + step_col * LATS + step_lat
        moved = lax.slice_in_dim(padded, moved_start, moved_start + width, axis=1)
        summed = summed + jnp.where(present[tap_index][None, :], moved, center)
    return -0.125 * summed


def rim_step(field, present, live):
    first_col = field[:, :LATS]
    last_col = lax.dynamic_slice_in_dim(field, (live - 1) * LATS, LATS, 1)
    from_prev = shifted(last_col, ("pix", "sub"), 1)
    from_next = shifted(first_col, ("pix", "sub"), -1)
    margin = LATS + 1
    channels = field.shape[0]
    padded = jnp.concatenate(
        [
            jnp.zeros((channels, margin), jnp.float32),
            from_prev,
            field,
            jnp.zeros((channels, LATS + margin), jnp.float32),
        ],
        axis=1,
    )
    padded = lax.dynamic_update_slice_in_dim(padded, from_next, margin + LATS + live * LATS, 1)
    return tap_sum(padded, present, margin + LATS, field.shape[1])


def shards(features, neighbours, live_cols, cheb_weight, out_bias):
    slot_count = features.shape[1]
    live = live_cols[0]
    own_slots = jnp.arange(slot_count, dtype=jnp.int32)[None, :]
    present = neighbours != LATS + own_slots
    terms = [features]
    older = features.astype(jnp.float32)
    newer = rim_step(older, present, live)
    terms.append(newer.astype(jnp.bfloat16))
    for degree in range(2, DEG + 1):
        upcoming = 2.0 * rim_step(newer, present, live) - older
        older, newer = (newer, upcoming)
        terms.append(newer.astype(jnp.bfloat16))
    share = slot_count // lax.axis_size("chan")
    summed = jnp.zeros((share, cheb_weight.shape[2]), jnp.float32)
    for degree in range(DEG + 1):
        piece = lax.all_to_all(terms[degree], "chan", split_axis=1, concat_axis=0, tiled=True)
        summed = summed + jnp.einsum(
            "ip,io->po", piece, cheb_weight[degree], preferred_element_type=jnp.float32
        )
    slots = lax.axis_index("chan") * share + jnp.arange(share, dtype=jnp.int32)
    alive = slots < live * LATS
    result = jnp.where(alive[:, None], summed + out_bias[None, :], 0.0)
    return result.astype(jnp.bfloat16).reshape(1, share, cheb_weight.shape[2])


def solution(mesh):
    in_specs = (
        P("chan", ("grp", "pix", "sub")),
        P(None, ("grp", "pix", "sub")),
        P(("grp", "pix", "sub")),
        P(),
        P(),
    )
    out_specs = P(("grp", "pix", "sub"), "chan", None)
    return jax.shard_map(shards, mesh=mesh, in_specs=in_specs, out_specs=out_specs, check_vma=False)
```

profile of v0, /device:TPU:0, one launch (start us, length us, event | category | flops | bytes accessed | tf_op | source)
XLA Modules:
  0.0 369.9 jit_solution(14855939197385692050)
XLA Ops:
  0.0 4.1 %copy.6 = bf16[128,8192]{0,1:T(8,128)(2,1)} copy(bf16[128,8192]{1,0:T(8,128)(2,1)} %param.5) | data formatting | bytes 4194304 | tf_op args[0]
  4.1 3.9 %convert_element_type.24 = f32[128,8192]{0,1:T(8,128)} convert(bf16[128,8192]{0,1:T(8,128)(2,1)} %copy.6) | non-fusion elementwise | flops 1048576 | bytes 6291456 | tf_op jit(solution)/shard_map/convert_element_type | solution.py:54
  8.6 0.9 constant_dynamic-slice_fusion.5
  9.5 0.5 collective-permute-start
  10.0 0.8 slice.341
  10.9 4.1 %collective-permute-start.1 = (f32[128,256]{0,1:T(8,128)S(1)}, f32[128,256]{0,1:T(8,128)S(1)}, u32[]{:S(2)}, u32[]{:S(2)}) collective-permute-start(f32[128,256]{0,1:T(8,128)S(1)} %slice.341), channel_id=1, source_target_pairs={{0,13},{1,0},{4,1},{5,4},{8,5},{9,8},{12,9},{13,12},{2,15},{3,2},{... | collective-permute-start | bytes 393224 | tf_op jit(solution)/shard_map/ppermute | solution.py:14
  15.0 0.7 slice_reduce_fusion.7
  15.7 1.0 collective-permute-done
  16.7 14.2 %concatenate.18 = f32[128,9218]{0,1:T(8,128)} concatenate(f32[128,257]{0,1:T(8,128)S(1)} %broadcast.29, f32[128,256]{0,1:T(8,128)S(1)} %collective-permute-done, bf16[128,8192]{0,1:T(8,128)(2,1)} %copy.6, f32[128,513]{0,1:T(8,128)S(1)} %broadcast.30), dimensions={1} | concatenate | bytes 7342080 | tf_op jit(solution)/shard_map/concatenate | solution.py:35
  30.9 1.7 dynamic_update_slice.18
  32.6 20.4 %fusion.81 = (bf16[128,8192]{0,1:T(8,128)(2,1)}, f32[128,8192]{0,1:T(8,128)S(1)}) fusion(f32[128,9218]{0,1:T(8,128)} %dynamic_update_slice.18, pred[8192]{0:T(1024)(128)(4,1)S(1)} %get-tuple-element.6, pred[8192]{0:T(1024)(128)(4,1)S(1)} %get-tuple-element.7, pred[8192]{0:T(1024)(128)(4,1)S(1)} %get-tuple-element.8, ...), kind=kLoop, calls=%fused_computation.148 | loop fusion | flops 17825792 | bytes 44105728 | tf_op jit(solution)/shard_map/convert_element_type | solution.py:56
  53.0 2.1 copy-done.3
  55.1 0.1 collective-permute-start.2
  55.2 3.5 collective-permute-start.3
  58.7 3.8 %all-to-all-start = ((bf16[128,2,4096]{0,2,1:T(8,128)(2,1)}), bf16[128,2,4096]{0,2,1:T(8,128)(2,1)S(1)}, u32[]{:S(2)}, u32[]{:S(2)}) async-start(bf16[128,2,4096]{0,2,1:T(8,128)(2,1)} %bitcast.1), calls=%async_computation | async-start | bytes 4194304 | tf_op jit(solution)/shard_map/all_to_all | solution.py:64
  62.5 14.5 %concatenate.19 = f32[128,9218]{0,1:T(8,128)} concatenate(f32[128,257]{0,1:T(8,128)S(1)} %broadcast.29, f32[128,256]{0,1:T(8,128)S(1)} %collective-permute-done.2, f32[128,8192]{0,1:T(8,128)} %copy-done.3, f32[128,513]{0,1:T(8,128)S(1)} %broadcast.30), dimensions={1} | concatenate | bytes 9439232 | tf_op jit(solution)/shard_map/concatenate | solution.py:35
  77.0 1.7 dynamic_update_slice.19
  78.7 20.9 %fusion.79 = (bf16[128,8192]{0,1:T(8,128)(2,1)}, f32[128,8192]{0,1:T(8,128)S(1)}) fusion(bf16[128,8192]{0,1:T(8,128)(2,1)} %copy.6, f32[128,9218]{0,1:T(8,128)} %dynamic_update_slice.19, pred[8192]{0:T(1024)(128)(4,1)S(1)} %get-tuple-element.6, pred[8192]{0:T(1024)(128)(4,1)S(1)} %get-tuple-element.7, pred[8192]{0:T(1024)(128)(4,1)S(1)} %get-tuple-element.8, ...), kind=kLoop, calls=%fused_computation.147 | loop fusion | flops 19922944 | bytes 46202880 | tf_op jit(solution)/shard_map/convert_element_type | solution.py:60
  99.5 2.0 copy-done.2
  101.5 0.1 collective-permute-start.4
  101.6 3.5 collective-permute-start.5
  105.1 3.1 collective-permute-done.4
  108.2 14.5 %concatenate.20 = f32[128,9218]{0,1:T(8,128)} concatenate(f32[128,257]{0,1:T(8,128)S(1)} %broadcast.29, f32[128,256]{0,1:T(8,128)S(1)} %collective-permute-done.4, f32[128,8192]{0,1:T(8,128)} %copy-done.2, f32[128,513]{0,1:T(8,128)S(1)} %broadcast.30), dimensions={1} | concatenate | bytes 9439232 | tf_op jit(solution)/shard_map/concatenate | solution.py:35
  122.7 1.7 dynamic_update_slice.20
  124.4 4.8 %all-to-all-start.1 = ((bf16[128,2,4096]{0,2,1:T(8,128)(2,1)}), bf16[128,2,4096]{0,2,1:T(8,128)(2,1)}, u32[]{:S(2)}, u32[]{:S(2)}) async-start(bf16[128,2,4096]{0,2,1:T(8,128)(2,1)} %bitcast.64), calls=%async_computation.1 | async-start | bytes 4194304 | tf_op jit(solution)/shard_map/all_to_all | solution.py:64
  129.2 21.3 %fusion.77 = (bf16[128,8192]{0,1:T(8,128)(2,1)}, f32[128,8192]{0,1:T(8,128)S(1)}) fusion(f32[128,8192]{0,1:T(8,128)} %copy-done.3, f32[128,9218]{0,1:T(8,128)} %dynamic_update_slice.20, pred[8192]{0:T(1024)(128)(4,1)S(1)} %get-tuple-element.6, pred[8192]{0:T(1024)(128)(4,1)S(1)} %get-tuple-element.7, pred[8192]{0:T(1024)(128)(4,1)S(1)} %get-tuple-element.8, ...), kind=kLoop, calls=%fused_computation.146 | loop fusion | flops 18874368 | bytes 48300032 | tf_op jit(solution)/shard_map/convert_element_type | solution.py:60
  150.5 2.1 copy-done
  152.7 3.5 collective-permute-start.7
  156.2 2.6 collective-permute-done.6
  158.9 14.5 %concatenate.21 = f32[128,9218]{0,1:T(8,128)} concatenate(f32[128,257]{0,1:T(8,128)S(1)} %broadcast.29, f32[128,256]{0,1:T(8,128)S(1)} %collective-permute-done.6, f32[128,8192]{0,1:T(8,128)} %copy-done, f32[128,513]{0,1:T(8,128)S(1)} %broadcast.30), dimensions={1} | concatenate | bytes 9439232 | tf_op jit(solution)/shard_map/concatenate | solution.py:35
  173.4 1.7 dynamic_update_slice.21
  175.0 3.8 %all-to-all-start.2 = ((bf16[128,2,4096]{0,2,1:T(8,128)(2,1)}), bf16[128,2,4096]{0,2,1:T(8,128)(2,1)S(1)}, u32[]{:S(2)}, u32[]{:S(2)}) async-start(bf16[128,2,4096]{0,2,1:T(8,128)(2,1)} %bitcast.10), calls=%async_computation.2 | async-start | bytes 4194304 | tf_op jit(solution)/shard_map/all_to_all | solution.py:64
  178.8 21.2 %fusion.75 = (bf16[128,8192]{0,1:T(8,128)(2,1)}, f32[128,8192]{0,1:T(8,128)S(1)}) fusion(f32[128,8192]{0,1:T(8,128)} %copy-done.2, f32[128,9218]{0,1:T(8,128)} %dynamic_update_slice.21, pred[8192]{0:T(1024)(128)(4,1)S(1)} %get-tuple-element.6, pred[8192]{0:T(1024)(128)(4,1)S(1)} %get-tuple-element.7, pred[8192]{0:T(1024)(128)(4,1)S(1)} %get-tuple-element.8, ...), kind=kLoop, calls=%fused_computation.145 | loop fusion | flops 18874368 | bytes 48300032 | tf_op jit(solution)/shard_map/convert_element_type | solution.py:60
  200.0 2.0 copy-done.1
  202.0 0.1 collective-permute-start.8
  202.1 3.5 collective-permute-start.9
  205.6 2.6 collective-permute-done.8
  208.3 14.5 %concatenate.22 = f32[128,9218]{0,1:T(8,128)} concatenate(f32[128,257]{0,1:T(8,128)S(1)} %broadcast.29, f32[128,256]{0,1:T(8,128)S(1)} %collective-permute-done.8, f32[128,8192]{0,1:T(8,128)} %copy-done.1, f32[128,513]{0,1:T(8,128)S(1)} %broadcast.30), dimensions={1} | concatenate | bytes 9439232 | tf_op jit(solution)/shard_map/concatenate | solution.py:35
  222.8 1.7 dynamic_update_slice.22
  224.4 4.8 %all-to-all-start.3 = ((bf16[128,2,4096]{0,2,1:T(8,128)(2,1)}), bf16[128,2,4096]{0,2,1:T(8,128)(2,1)}, u32[]{:S(2)}, u32[]{:S(2)}) async-start(bf16[128,2,4096]{0,2,1:T(8,128)(2,1)} %bitcast.14), calls=%async_computation.3 | async-start | bytes 4194304 | tf_op jit(solution)/shard_map/all_to_all | solution.py:64
  229.3 21.4 %fusion.73 = (bf16[128,8192]{0,1:T(8,128)(2,1)}, f32[128,8192]{0,1:T(8,128)S(1)}) fusion(f32[128,8192]{0,1:T(8,128)} %copy-done, f32[128,9218]{0,1:T(8,128)} %dynamic_update_slice.22, pred[8192]{0:T(1024)(128)(4,1)S(1)} %get-tuple-element.6, pred[8192]{0:T(1024)(128)(4,1)S(1)} %get-tuple-element.7, pred[8192]{0:T(1024)(128)(4,1)S(1)} %get-tuple-element.8, ...), kind=kLoop, calls=%fused_computation.144 | loop fusion | flops 18874368 | bytes 48300032 | tf_op jit(solution)/shard_map/convert_element_type | solution.py:60
  250.7 2.1 copy-done.4
  252.8 3.5 collective-permute-start.11
  256.4 2.6 collective-permute-done.10
  259.0 14.5 %concatenate.23 = f32[128,9218]{0,1:T(8,128)} concatenate(f32[128,257]{0,1:T(8,128)S(1)} %broadcast.29, f32[128,256]{0,1:T(8,128)S(1)} %collective-permute-done.10, f32[128,8192]{0,1:T(8,128)} %copy-done.4, f32[128,513]{0,1:T(8,128)S(1)} %broadcast.30), dimensions={1} | concatenate | bytes 9439232 | tf_op jit(solution)/shard_map/concatenate | solution.py:35
  273.5 1.7 dynamic_update_slice.23
  275.2 4.8 %all-to-all-start.4 = ((bf16[128,2,4096]{0,2,1:T(8,128)(2,1)}), bf16[128,2,4096]{0,2,1:T(8,128)(2,1)}, u32[]{:S(2)}, u32[]{:S(2)}) async-start(bf16[128,2,4096]{0,2,1:T(8,128)(2,1)} %bitcast.18), calls=%async_computation.4 | async-start | bytes 4194304 | tf_op jit(solution)/shard_map/all_to_all | solution.py:64
  280.0 21.2 %fusion.7 = bf16[128,8192]{0,1:T(8,128)(2,1)} fusion(f32[128,8192]{0,1:T(8,128)} %copy-done.1, f32[128,9218]{0,1:T(8,128)} %dynamic_update_slice.23, pred[8192]{0:T(1024)(128)(4,1)S(1)} %get-tuple-element.6, pred[8192]{0:T(1024)(128)(4,1)S(1)} %get-tuple-element.7, pred[8192]{0:T(1024)(128)(4,1)S(1)} %get-tuple-element.8, ...), kind=kLoop, calls=%fused_computation.14 | loop fusion | flops 18874368 | bytes 44105728 | tf_op jit(solution)/shard_map/convert_element_type | solution.py:60
  301.2 3.0 copy.7
  304.2 5.0 %all-to-all-start.5 = ((bf16[128,2,4096]{0,2,1:T(8,128)(2,1)}), bf16[128,2,4096]{0,2,1:T(8,128)(2,1)}, u32[]{:S(2)}, u32[]{:S(2)}) async-start(bf16[128,2,4096]{0,2,1:T(8,128)(2,1)} %bitcast.54), calls=%async_computation.5 | async-start | bytes 4194304 | tf_op jit(solution)/shard_map/all_to_all | solution.py:64
  309.2 2.7 fusion.64
  311.9 4.1 %copy.9 = bf16[2,128,4096]{2,1,0:T(8,128)(2,1)} copy(bf16[2,128,4096]{1,2,0:T(8,128)(2,1)} %bitcast.7) | data formatting | bytes 4194304 | tf_op jit(solution)/shard_map/all_to_all | solution.py:64
  316.0 5.7 %convolution_add_fusion.5 = f32[4096,256]{1,0:T(8,128)} fusion(f32[4096,256]{1,0:T(8,128)} %fusion.64, bf16[256,4096]{1,0:T(8,128)(2,1)} %bitcast.60, bf16[7,256,256]{2,1,0:T(8,128)(2,1)S(1)} %copy-done.8), kind=kOutput, calls=%fused_computation.7 | convolution fusion | flops 537919488 | bytes 10616832 | tf_op jit(solution)/shard_map/ip,io->po/dot_general | solution.py:65
  321.7 2.7 copy.10
  324.4 5.5 %convolution_add_fusion.4 = f32[4096,256]{1,0:T(8,128)} fusion(f32[4096,256]{1,0:T(8,128)} %convolution_add_fusion.5, bf16[256,4096]{1,0:T(8,128)(2,1)} %bitcast.61, bf16[7,256,256]{2,1,0:T(8,128)(2,1)S(1)} %copy-done.8), kind=kOutput, calls=%fused_computation.6 | convolution fusion | flops 537919488 | bytes 10616832 | tf_op jit(solution)/shard_map/ip,io->po/dot_general | solution.py:65
  329.9 4.1 %copy.11 = bf16[2,128,4096]{2,1,0:T(8,128)(2,1)} copy(bf16[2,128,4096]{1,2,0:T(8,128)(2,1)} %bitcast.15) | data formatting | bytes 4194304 | tf_op jit(solution)/shard_map/all_to_all | solution.py:64
  334.0 3.8 %all-to-all-start.6 = ((bf16[128,2,4096]{0,2,1:T(8,128)(2,1)}), bf16[128,2,4096]{0,2,1:T(8,128)(2,1)S(1)}, u32[]{:S(2)}, u32[]{:S(2)}) async-start(bf16[128,2,4096]{0,2,1:T(8,128)(2,1)} %bitcast.65), calls=%async_computation.6 | async-start | bytes 4194304 | tf_op jit(solution)/shard_map/all_to_all | solution.py:64
  337.8 5.5 %convolution_add_fusion.3 = f32[4096,256]{1,0:T(8,128)} fusion(f32[4096,256]{1,0:T(8,128)} %convolution_add_fusion.4, bf16[256,4096]{1,0:T(8,128)(2,1)} %bitcast.58, bf16[7,256,256]{2,1,0:T(8,128)(2,1)S(1)} %copy-done.8), kind=kOutput, calls=%fused_computation.5 | convolution fusion | flops 537919488 | bytes 10616832 | tf_op jit(solution)/shard_map/ip,io->po/dot_general | solution.py:65
  343.3 4.1 %copy.12 = bf16[2,128,4096]{2,1,0:T(8,128)(2,1)} copy(bf16[2,128,4096]{1,2,0:T(8,128)(2,1)} %bitcast.19) | data formatting | bytes 4194304 | tf_op jit(solution)/shard_map/all_to_all | solution.py:64
  347.4 5.5 %convolution_add_fusion.2 = f32[4096,256]{1,0:T(8,128)} fusion(f32[4096,256]{1,0:T(8,128)} %convolution_add_fusion.3, bf16[256,4096]{1,0:T(8,128)(2,1)} %bitcast.62, bf16[7,256,256]{2,1,0:T(8,128)(2,1)S(1)} %copy-done.8), kind=kOutput, calls=%fused_computation.4 | convolution fusion | flops 537919488 | bytes 10616832 | tf_op jit(solution)/shard_map/ip,io->po/dot_general | solution.py:65
  352.9 4.1 %copy.13 = bf16[2,128,4096]{2,1,0:T(8,128)(2,1)} copy(bf16[2,128,4096]{1,2,0:T(8,128)(2,1)} %bitcast.23) | data formatting | bytes 4194304 | tf_op jit(solution)/shard_map/all_to_all | solution.py:64
  357.0 5.5 %convolution_add_fusion.1 = f32[4096,256]{1,0:T(8,128)} fusion(f32[4096,256]{1,0:T(8,128)} %convolution_add_fusion.2, bf16[256,4096]{1,0:T(8,128)(2,1)} %bitcast.63, bf16[7,256,256]{2,1,0:T(8,128)(2,1)S(1)} %copy-done.8), kind=kOutput, calls=%fused_computation.3 | convolution fusion | flops 537919488 | bytes 10616832 | tf_op jit(solution)/shard_map/ip,io->po/dot_general | solution.py:65
  362.5 2.8 copy.14
  365.3 4.5 %fusion.3 = bf16[1,4096,256]{2,1,0:T(8,128)(2,1)} fusion(f32[4096,256]{1,0:T(8,128)} %convolution_add_fusion.1, bf16[256,4096]{1,0:T(8,128)(2,1)} %bitcast.59, f32[256]{0:T(256)S(1)} %copy-done.10, pred[4096]{0:T(1024)(128)(4,1)S(1)} %add_compare_fusion, bf16[7,256,256]{2,1,0:T(8,128)(2,1)S(1)} %copy-done.8), kind=kOutput, calls=%fused_computation.9 | convolution fusion | flops 541065216 | bytes 8524800 | tf_op jit(solution)/shard_map/ip,io->po/dot_general | solution.py:65
  (43 shorter events, 0.4 us)
Async XLA Ops:
  4.1 10.9 %copy-start.9 = (s32[8,8192]{1,0:T(8,128)S(1)}, s32[8,8192]{1,0:T(8,128)}, u32[]{:S(2)}) copy-start(s32[8,8192]{1,0:T(8,128)} %param.6) | copy-start | bytes 786436
  9.5 7.2 %collective-permute-start = (f32[128,256]{0,1:T(8,128)S(1)}, f32[128,256]{0,1:T(8,128)S(1)}, u32[]{:S(2)}, u32[]{:S(2)}) collective-permute-start(f32[128,256]{0,1:T(8,128)S(1)} %constant_dynamic-slice_fusion.5), channel_id=1, source_target_pairs={{0,1},{1,4},{4,5},{5,8},{8,9},{9,12},{12,13},{13,0},{2,3},{3,6},{6... | collective-permute-start | bytes 393224 | tf_op jit(solution)/shard_map/ppermute | solution.py:14
  10.9 20.1 %collective-permute-start.1 = (f32[128,256]{0,1:T(8,128)S(1)}, f32[128,256]{0,1:T(8,128)S(1)}, u32[]{:S(2)}, u32[]{:S(2)}) collective-permute-start(f32[128,256]{0,1:T(8,128)S(1)} %slice.341), channel_id=1, source_target_pairs={{0,13},{1,0},{4,1},{5,4},{8,5},{9,8},{12,9},{13,12},{2,15},{3,2},{... | collective-permute-start | bytes 393224 | tf_op jit(solution)/shard_map/ppermute | solution.py:14
  53.0 2.1 copy-start.3
  55.1 7.4 %collective-permute-start.2 = (f32[128,256]{0,1:T(8,128)S(1)}, f32[128,256]{0,1:T(8,128)S(1)}, u32[]{:S(2)}, u32[]{:S(2)}) collective-permute-start(f32[128,256]{0,1:T(8,128)S(1)} %get-tuple-element.32), channel_id=1, source_target_pairs={{0,1},{1,4},{4,5},{5,8},{8,9},{9,12},{12,13},{13,0},{2,3},{3,6},{6... | collective-permute-start | bytes 393224 | tf_op jit(solution)/shard_map/ppermute | solution.py:14
  55.2 21.8 %collective-permute-start.3 = (f32[128,256]{0,1:T(8,128)S(1)}, f32[128,256]{0,1:T(8,128)S(1)}, u32[]{:S(2)}, u32[]{:S(2)}) collective-permute-start(f32[128,256]{0,1:T(8,128)S(1)} %get-tuple-element.31), channel_id=1, source_target_pairs={{0,13},{1,0},{4,1},{5,4},{8,5},{9,8},{12,9},{13,12},{2,15},{3,2},{... | collective-permute-start | bytes 393224 | tf_op jit(solution)/shard_map/ppermute | solution.py:14
  58.7 65.7 %all-to-all-start = ((bf16[128,2,4096]{0,2,1:T(8,128)(2,1)}), bf16[128,2,4096]{0,2,1:T(8,128)(2,1)S(1)}, u32[]{:S(2)}, u32[]{:S(2)}) async-start(bf16[128,2,4096]{0,2,1:T(8,128)(2,1)} %bitcast.1), calls=%async_computation | async-start | bytes 4194304 | tf_op jit(solution)/shard_map/all_to_all | solution.py:64
  99.5 2.0 copy-start.2
  101.5 6.6 %collective-permute-start.4 = (f32[128,256]{0,1:T(8,128)S(1)}, f32[128,256]{0,1:T(8,128)S(1)}, u32[]{:S(2)}, u32[]{:S(2)}) collective-permute-start(f32[128,256]{0,1:T(8,128)S(1)} %get-tuple-element.30), channel_id=1, source_target_pairs={{0,1},{1,4},{4,5},{5,8},{8,9},{9,12},{12,13},{13,0},{2,3},{3,6},{6... | collective-permute-start | bytes 393224 | tf_op jit(solution)/shard_map/ppermute | solution.py:14
  101.6 21.1 %collective-permute-start.5 = (f32[128,256]{0,1:T(8,128)S(1)}, f32[128,256]{0,1:T(8,128)S(1)}, u32[]{:S(2)}, u32[]{:S(2)}) collective-permute-start(f32[128,256]{0,1:T(8,128)S(1)} %get-tuple-element.29), channel_id=1, source_target_pairs={{0,13},{1,0},{4,1},{5,4},{8,5},{9,8},{12,9},{13,12},{2,15},{3,2},{... | collective-permute-start | bytes 393224 | tf_op jit(solution)/shard_map/ppermute | solution.py:14
  124.4 26.2 %copy-start.5 = (bf16[128,2,4096]{0,2,1:T(8,128)(2,1)}, bf16[128,2,4096]{0,2,1:T(8,128)(2,1)S(1)}, u32[]{:S(2)}) copy-start(bf16[128,2,4096]{0,2,1:T(8,128)(2,1)S(1)} %all-to-all-done) | copy-start | bytes 6291460
  124.4 50.7 %all-to-all-start.1 = ((bf16[128,2,4096]{0,2,1:T(8,128)(2,1)}), bf16[128,2,4096]{0,2,1:T(8,128)(2,1)}, u32[]{:S(2)}, u32[]{:S(2)}) async-start(bf16[128,2,4096]{0,2,1:T(8,128)(2,1)} %bitcast.64), calls=%async_computation.1 | async-start | bytes 4194304 | tf_op jit(solution)/shard_map/all_to_all | solution.py:64
  150.5 2.1 copy-start
  152.6 6.2 %collective-permute-start.6 = (f32[128,256]{0,1:T(8,128)S(1)}, f32[128,256]{0,1:T(8,128)S(1)}, u32[]{:S(2)}, u32[]{:S(2)}) collective-permute-start(f32[128,256]{0,1:T(8,128)S(1)} %get-tuple-element.28), channel_id=1, source_target_pairs={{0,1},{1,4},{4,5},{5,8},{8,9},{9,12},{12,13},{13,0},{2,3},{3,6},{6... | collective-permute-start | bytes 393224 | tf_op jit(solution)/shard_map/ppermute | solution.py:14
  152.7 20.7 %collective-permute-start.7 = (f32[128,256]{0,1:T(8,128)S(1)}, f32[128,256]{0,1:T(8,128)S(1)}, u32[]{:S(2)}, u32[]{:S(2)}) collective-permute-start(f32[128,256]{0,1:T(8,128)S(1)} %get-tuple-element.27), channel_id=1, source_target_pairs={{0,13},{1,0},{4,1},{5,4},{8,5},{9,8},{12,9},{13,12},{2,15},{3,2},{... | collective-permute-start | bytes 393224 | tf_op jit(solution)/shard_map/ppermute | solution.py:14
  175.0 49.4 %all-to-all-start.2 = ((bf16[128,2,4096]{0,2,1:T(8,128)(2,1)}), bf16[128,2,4096]{0,2,1:T(8,128)(2,1)S(1)}, u32[]{:S(2)}, u32[]{:S(2)}) async-start(bf16[128,2,4096]{0,2,1:T(8,128)(2,1)} %bitcast.10), calls=%async_computation.2 | async-start | bytes 4194304 | tf_op jit(solution)/shard_map/all_to_all | solution.py:64
  200.0 2.0 copy-start.1
  202.0 6.2 %collective-permute-start.8 = (f32[128,256]{0,1:T(8,128)S(1)}, f32[128,256]{0,1:T(8,128)S(1)}, u32[]{:S(2)}, u32[]{:S(2)}) collective-permute-start(f32[128,256]{0,1:T(8,128)S(1)} %get-tuple-element.26), channel_id=1, source_target_pairs={{0,1},{1,4},{4,5},{5,8},{8,9},{9,12},{12,13},{13,0},{2,3},{3,6},{6... | collective-permute-start | bytes 393224 | tf_op jit(solution)/shard_map/ppermute | solution.py:14
  202.1 20.7 %collective-permute-start.9 = (f32[128,256]{0,1:T(8,128)S(1)}, f32[128,256]{0,1:T(8,128)S(1)}, u32[]{:S(2)}, u32[]{:S(2)}) collective-permute-start(f32[128,256]{0,1:T(8,128)S(1)} %get-tuple-element.25), channel_id=1, source_target_pairs={{0,13},{1,0},{4,1},{5,4},{8,5},{9,8},{12,9},{13,12},{2,15},{3,2},{... | collective-permute-start | bytes 393224 | tf_op jit(solution)/shard_map/ppermute | solution.py:14
  224.4 26.2 %copy-start.6 = (bf16[128,2,4096]{0,2,1:T(8,128)(2,1)}, bf16[128,2,4096]{0,2,1:T(8,128)(2,1)S(1)}, u32[]{:S(2)}) copy-start(bf16[128,2,4096]{0,2,1:T(8,128)(2,1)S(1)} %all-to-all-done.2) | copy-start | bytes 6291460
  224.4 50.7 %all-to-all-start.3 = ((bf16[128,2,4096]{0,2,1:T(8,128)(2,1)}), bf16[128,2,4096]{0,2,1:T(8,128)(2,1)}, u32[]{:S(2)}, u32[]{:S(2)}) async-start(bf16[128,2,4096]{0,2,1:T(8,128)(2,1)} %bitcast.14), calls=%async_computation.3 | async-start | bytes 4194304 | tf_op jit(solution)/shard_map/all_to_all | solution.py:64
  250.7 2.1 copy-start.4
  252.7 6.2 %collective-permute-start.10 = (f32[128,256]{0,1:T(8,128)S(1)}, f32[128,256]{0,1:T(8,128)S(1)}, u32[]{:S(2)}, u32[]{:S(2)}) collective-permute-start(f32[128,256]{0,1:T(8,128)S(1)} %get-tuple-element.24), channel_id=1, source_target_pairs={{0,1},{1,4},{4,5},{5,8},{8,9},{9,12},{12,13},{13,0},{2,3},{3,6},{6... | collective-permute-start | bytes 393224 | tf_op jit(solution)/shard_map/ppermute | solution.py:14
  252.8 20.7 %collective-permute-start.11 = (f32[128,256]{0,1:T(8,128)S(1)}, f32[128,256]{0,1:T(8,128)S(1)}, u32[]{:S(2)}, u32[]{:S(2)}) collective-permute-start(f32[128,256]{0,1:T(8,128)S(1)} %get-tuple-element.23), channel_id=1, source_target_pairs={{0,13},{1,0},{4,1},{5,4},{8,5},{9,8},{12,9},{13,12},{2,15},{3,2},{... | collective-permute-start | bytes 393224 | tf_op jit(solution)/shard_map/ppermute | solution.py:14
  275.2 29.0 %all-to-all-start.4 = ((bf16[128,2,4096]{0,2,1:T(8,128)(2,1)}), bf16[128,2,4096]{0,2,1:T(8,128)(2,1)}, u32[]{:S(2)}, u32[]{:S(2)}) async-start(bf16[128,2,4096]{0,2,1:T(8,128)(2,1)} %bitcast.18), calls=%async_computation.4 | async-start | bytes 4194304 | tf_op jit(solution)/shard_map/all_to_all | solution.py:64
  301.1 8.0 %copy-start.8 = (bf16[7,256,256]{2,1,0:T(8,128)(2,1)S(1)}, bf16[7,256,256]{2,1,0:T(8,128)(2,1)}, u32[]{:S(2)}) copy-start(bf16[7,256,256]{2,1,0:T(8,128)(2,1)} %param.8) | copy-start | bytes 2752516
  304.2 29.8 %all-to-all-start.5 = ((bf16[128,2,4096]{0,2,1:T(8,128)(2,1)}), bf16[128,2,4096]{0,2,1:T(8,128)(2,1)}, u32[]{:S(2)}, u32[]{:S(2)}) async-start(bf16[128,2,4096]{0,2,1:T(8,128)(2,1)} %bitcast.54), calls=%async_computation.5 | async-start | bytes 4194304 | tf_op jit(solution)/shard_map/all_to_all | solution.py:64
  316.0 5.7 %copy-start.7 = (bf16[128,2,4096]{0,2,1:T(8,128)(2,1)S(1)}, bf16[128,2,4096]{0,2,1:T(8,128)(2,1)}, u32[]{:S(2)}) copy-start(bf16[128,2,4096]{0,2,1:T(8,128)(2,1)} %copy-done.6) | copy-start | bytes 6291460
  334.0 28.6 %all-to-all-start.6 = ((bf16[128,2,4096]{0,2,1:T(8,128)(2,1)}), bf16[128,2,4096]{0,2,1:T(8,128)(2,1)S(1)}, u32[]{:S(2)}, u32[]{:S(2)}) async-start(bf16[128,2,4096]{0,2,1:T(8,128)(2,1)} %bitcast.65), calls=%async_computation.6 | async-start | bytes 4194304 | tf_op jit(solution)/shard_map/all_to_all | solution.py:64
  362.5 2.8 copy-start.10
where the time goes:
time: 373 us; the launch traced here: 370 us
  local copies, waits for them, and re-layouts  138 us (37%)
  other arithmetic  130 us (35%)
  starting transfers between devices  53.3 us (14%)
  matrix products  35.1 us (9%)
  waiting for transfers between devices  12 us (3%)
    convert_element_type x6, other arithmetic, shards(): terms.append(newer.astype(jnp.bfloat16))  126 us
    concatenate x6, local copies, waits for them, and re-layouts, rim_step(): jnp.concatenate([jnp.zeros((channels, margin), jnp.float32), from_prev, f...  86.6 us
    dot_general x7, matrix products, shards(): jnp.einsum('ip,io->po', piece, cheb_weight[degree], preferred_element_typ...  35.1 us
    all_to_all x7, starting transfers between devices, shards(): lax.all_to_all(terms[degree], 'chan', split_axis=1, concat_axis=0, tiled=...  30.7 us
    all_to_all x7, local copies, waits for them, and re-layouts, shards(): lax.all_to_all(terms[degree], 'chan', split_axis=1, concat_axis=0, tiled=...  24.8 us
    ppermute x12, starting transfers between devices, shifted(): return lax.ppermute(value, axis, pairs)  22.6 us
    unnamed x23, local copies, waits for them, and re-layouts  14.2 us
    ppermute x12, waiting for transfers between devices, shifted(): return lax.ppermute(value, axis, pairs)  12 us
  transfers between devices with their start and end apart: 19, of which 5 were waited for; matrix products, arithmetic and copies ran while one was open for 69% of the time, Pallas kernels for 0%

commit v1 on v0

--- a/solution.py
+++ b/solution.py
@@ -61,7 +61,12 @@
     share = slot_count // lax.axis_size("chan")
     summed = jnp.zeros((share, cheb_weight.shape[2]), jnp.float32)
     for degree in range(DEG + 1):
-        piece = lax.all_to_all(terms[degree], "chan", split_axis=1, concat_axis=0, tiled=True)
+        piece = jnp.concatenate(
+            lax.all_to_all(
+                jnp.stack(jnp.split(terms[degree], lax.axis_size("chan"), axis=1)), "chan", 0, 0
+            ),
+            axis=0,
+        )
         summed = summed + jnp.einsum(
             "ip,io->po", piece, cheb_weight[degree], preferred_element_type=jnp.float32
         )

time: 373 us -> 341 us (0.914)
  the two profiles are of different devices: /device:TPU:0 before, /device:TPU:28 now
where the time goes in v1:
time: 341 us; the launch traced here: 339 us
  other arithmetic  123 us (36%)
  waiting for transfers between devices  76.9 us (23%)
  local copies, waits for them, and re-layouts  64.7 us (19%)
  starting transfers between devices  50.3 us (15%)
  matrix products  23.5 us (7%)
    convert_element_type x6, other arithmetic, shards(): terms.append(newer.astype(jnp.bfloat16))  110 us
    all_to_all x7, waiting for transfers between devices, shards(): lax.all_to_all(jnp.stack(jnp.split(terms[degree], lax.axis_size('chan'),...  72.8 us
    concatenate x6, local copies, waits for them, and re-layouts, rim_step(): jnp.concatenate([jnp.zeros((channels, margin), jnp.float32), from_prev, f...  38 us
    all_to_all x7, starting transfers between devices, shards(): lax.all_to_all(jnp.stack(jnp.split(terms[degree], lax.axis_size('chan'),...  33.2 us
    dot_general x7, matrix products, shards(): jnp.einsum('ip,io->po', piece, cheb_weight[degree], preferred_element_typ...  23.5 us
    ppermute x12, starting transfers between devices, shifted(): return lax.ppermute(value, axis, pairs)  17.2 us
    another operation x7, local copies, waits for them, and re-layouts, shards(): jnp.stack(jnp.split(terms[degree], lax.axis_size('chan'), axis=1))  11.8 us
    dynamic_update_slice x6, local copies, waits for them, and re-layouts, rim_step(): lax.dynamic_update_slice_in_dim(padded, from_next, margin + LATS + live *...  11.1 us
  transfers between devices with their start and end apart: 19, of which 9 were waited for; matrix products, arithmetic and copies ran while one was open for 59% of the time, Pallas kernels for 0%

profile of v1, /device:TPU:28, one launch (start us, length us, event | category | flops | bytes accessed | tf_op | source)
XLA Modules:
  0.0 339.1 jit_solution(10171591011631306809)
XLA Ops:
  0.0 1.7 slice_bitcast_fusion.13
  1.7 1.5 pad_maximum_fusion
  3.2 4.8 %all-to-all-start = ((bf16[2,128,4096]{2,1,0:T(8,128)(2,1)}), bf16[2,128,4096]{2,1,0:T(8,128)(2,1)}, u32[]{:S(2)}, u32[]{:S(2)}) async-start(bf16[2,128,4096]{2,1,0:T(8,128)(2,1)} %pad_maximum_fusion), calls=%async_computation | async-start | bytes 4194304 | tf_op jit(solution)/shard_map/all_to_all | solution.py:65
  8.0 2.4 convert_element_type.24
  11.1 0.9 constant_dynamic-slice_fusion.5
  12.1 1.8 collective-permute-start.1
  13.9 0.7 slice_reduce_fusion.7
  14.6 1.8 collective-permute-done
  16.5 4.3 %concatenate.18 = f32[128,9218]{1,0:T(8,128)} concatenate(f32[128,257]{1,0:T(8,128)S(1)} %broadcast.29, f32[128,256]{1,0:T(8,128)S(1)} %collective-permute-done, bf16[128,8192]{1,0:T(8,128)(2,1)S(1)} %copy-done.4, f32[128,513]{1,0:T(8,128)S(1)} %broadcast.30), dimensions={1} | concatenate | bytes 7342080 | tf_op jit(solution)/shard_map/concatenate | solution.py:35
  20.8 1.8 dynamic_update_slice.18
  22.7 16.7 %fusion.81 = (bf16[128,8192]{1,0:T(8,128)(2,1)S(1)}, f32[128,8192]{1,0:T(8,128)S(1)}) fusion(f32[128,9218]{1,0:T(8,128)} %dynamic_update_slice.18, pred[8192]{0:T(1024)(128)(4,1)S(1)} %get-tuple-element.6, pred[8192]{0:T(1024)(128)(4,1)S(1)} %get-tuple-element.7, pred[8192]{0:T(1024)(128)(4,1)S(1)} %get-tuple-element.8, ...), kind=kLoop, calls=%fused_computation.169 | loop fusion | flops 17825792 | bytes 44105728 | tf_op jit(solution)/shard_map/convert_element_type | solution.py:56
  39.4 0.2 slice_bitcast_fusion.11
  39.7 1.7 collective-permute-start.3
  41.4 1.5 pad_maximum_fusion.1
  42.9 1.2 collective-permute-done.2
  44.1 6.7 %concatenate.19 = f32[128,9218]{1,0:T(8,128)} concatenate(f32[128,257]{1,0:T(8,128)S(1)} %broadcast.29, f32[128,256]{1,0:T(8,128)S(1)} %collective-permute-done.2, f32[128,8192]{1,0:T(8,128)} %copy-done.3, f32[128,513]{1,0:T(8,128)S(1)} %broadcast.30), dimensions={1} | concatenate | bytes 9439232 | tf_op jit(solution)/shard_map/concatenate | solution.py:35
  50.8 1.8 dynamic_update_slice.19
  52.6 17.7 %fusion.79 = (bf16[128,8192]{1,0:T(8,128)(2,1)}, f32[128,8192]{1,0:T(8,128)S(1)}) fusion(bf16[128,8192]{1,0:T(8,128)(2,1)S(1)} %copy-done.4, f32[128,9218]{1,0:T(8,128)} %dynamic_update_slice.19, pred[8192]{0:T(1024)(128)(4,1)S(1)} %get-tuple-element.6, pred[8192]{0:T(1024)(128)(4,1)S(1)} %get-tuple-element.7, pred[8192]{0:T(1024)(128)(4,1)S(1)} %get-tuple-element.8, ...), kind=kLoop, calls=%fused_computation.168 | loop fusion | flops 19922944 | bytes 46202880 | tf_op jit(solution)/shard_map/convert_element_type | solution.py:60
  70.3 3.2 slice_bitcast_fusion.9
  73.6 1.0 collective-permute-start.4
  74.6 0.8 collective-permute-start.5
  75.4 1.5 pad_maximum_fusion.2
  76.9 1.1 collective-permute-done.4
  78.0 6.7 %concatenate.20 = f32[128,9218]{1,0:T(8,128)} concatenate(f32[128,257]{1,0:T(8,128)S(1)} %broadcast.29, f32[128,256]{1,0:T(8,128)S(1)} %collective-permute-done.4, f32[128,8192]{1,0:T(8,128)} %copy-done.2, f32[128,513]{1,0:T(8,128)S(1)} %broadcast.30), dimensions={1} | concatenate | bytes 9439232 | tf_op jit(solution)/shard_map/concatenate | solution.py:35
  84.7 1.8 dynamic_update_slice.20
  86.6 18.7 %fusion.77 = (bf16[128,8192]{1,0:T(8,128)(2,1)}, f32[128,8192]{1,0:T(8,128)S(1)}) fusion(f32[128,8192]{1,0:T(8,128)} %copy-done.3, f32[128,9218]{1,0:T(8,128)} %dynamic_update_slice.20, pred[8192]{0:T(1024)(128)(4,1)S(1)} %get-tuple-element.6, pred[8192]{0:T(1024)(128)(4,1)S(1)} %get-tuple-element.7, pred[8192]{0:T(1024)(128)(4,1)S(1)} %get-tuple-element.8, ...), kind=kLoop, calls=%fused_computation.167 | loop fusion | flops 18874368 | bytes 48300032 | tf_op jit(solution)/shard_map/convert_element_type | solution.py:60
  105.3 3.2 slice_bitcast_fusion.7
  108.6 2.8 collective-permute-start.6
  111.4 1.5 pad_maximum_fusion.3
  113.0 6.7 %concatenate.21 = f32[128,9218]{1,0:T(8,128)} concatenate(f32[128,257]{1,0:T(8,128)S(1)} %broadcast.29, f32[128,256]{1,0:T(8,128)S(1)} %collective-permute-done.6, f32[128,8192]{1,0:T(8,128)} %copy-done, f32[128,513]{1,0:T(8,128)S(1)} %broadcast.30), dimensions={1} | concatenate | bytes 9439232 | tf_op jit(solution)/shard_map/concatenate | solution.py:35
  119.7 1.8 dynamic_update_slice.21
  121.6 18.9 %fusion.75 = (bf16[128,8192]{1,0:T(8,128)(2,1)}, f32[128,8192]{1,0:T(8,128)S(1)}) fusion(f32[128,8192]{1,0:T(8,128)} %copy-done.2, f32[128,9218]{1,0:T(8,128)} %dynamic_update_slice.21, pred[8192]{0:T(1024)(128)(4,1)S(1)} %get-tuple-element.6, pred[8192]{0:T(1024)(128)(4,1)S(1)} %get-tuple-element.7, pred[8192]{0:T(1024)(128)(4,1)S(1)} %get-tuple-element.8, ...), kind=kLoop, calls=%fused_computation.166 | loop fusion | flops 18874368 | bytes 48300032 | tf_op jit(solution)/shard_map/convert_element_type | solution.py:60
  140.5 4.6 %collective-permute-start.8 = (f32[128,256]{1,0:T(8,128)S(1)}, f32[128,256]{1,0:T(8,128)S(1)}, u32[]{:S(2)}, u32[]{:S(2)}) collective-permute-start(f32[128,256]{1,0:T(8,128)S(1)} %get-tuple-element.26), channel_id=1, source_target_pairs={{0,1},{1,4},{4,5},{5,8},{8,9},{9,12},{12,13},{13,0},{2,3},{3,6},{6... | collective-permute-start | bytes 393224 | tf_op jit(solution)/shard_map/ppermute | solution.py:14
  145.1 1.7 slice_bitcast_fusion.5
  146.8 1.5 pad_maximum_fusion.4
  148.3 6.8 %concatenate.22 = f32[128,9218]{1,0:T(8,128)} concatenate(f32[128,257]{1,0:T(8,128)S(1)} %broadcast.29, f32[128,256]{1,0:T(8,128)S(1)} %collective-permute-done.8, f32[128,8192]{1,0:T(8,128)} %copy-done.1, f32[128,513]{1,0:T(8,128)S(1)} %broadcast.30), dimensions={1} | concatenate | bytes 9439232 | tf_op jit(solution)/shard_map/concatenate | solution.py:35
  155.1 1.8 dynamic_update_slice.22
  156.9 5.0 %all-to-all-start.1 = ((bf16[2,128,4096]{2,1,0:T(8,128)(2,1)}), bf16[2,128,4096]{2,1,0:T(8,128)(2,1)}, u32[]{:S(2)}, u32[]{:S(2)}) async-start(bf16[2,128,4096]{2,1,0:T(8,128)(2,1)} %pad_maximum_fusion.1), calls=%async_computation.1 | async-start | bytes 4194304 | tf_op jit(solution)/shard_map/all_to_all | solution.py:65
  162.0 18.7 %fusion.73 = (bf16[128,8192]{1,0:T(8,128)(2,1)}, f32[128,8192]{1,0:T(8,128)S(1)}) fusion(f32[128,8192]{1,0:T(8,128)} %copy-done, f32[128,9218]{1,0:T(8,128)} %dynamic_update_slice.22, pred[8192]{0:T(1024)(128)(4,1)S(1)} %get-tuple-element.6, pred[8192]{0:T(1024)(128)(4,1)S(1)} %get-tuple-element.7, pred[8192]{0:T(1024)(128)(4,1)S(1)} %get-tuple-element.8, ...), kind=kLoop, calls=%fused_computation.165 | loop fusion | flops 18874368 | bytes 48300032 | tf_op jit(solution)/shard_map/convert_element_type | solution.py:60
  180.7 2.1 copy-done.5
  182.8 4.3 %collective-permute-start.10 = (f32[128,256]{1,0:T(8,128)S(1)}, f32[128,256]{1,0:T(8,128)S(1)}, u32[]{:S(2)}, u32[]{:S(2)}) collective-permute-start(f32[128,256]{1,0:T(8,128)S(1)} %get-tuple-element.24), channel_id=1, source_target_pairs={{0,1},{1,4},{4,5},{5,8},{8,9},{9,12},{12,13},{13,0},{2,3},{3,6},{6... | collective-permute-start | bytes 393224 | tf_op jit(solution)/shard_map/ppermute | solution.py:14
  187.1 4.8 %all-to-all-start.2 = ((bf16[2,128,4096]{2,1,0:T(8,128)(2,1)}), bf16[2,128,4096]{2,1,0:T(8,128)(2,1)}, u32[]{:S(2)}, u32[]{:S(2)}) async-start(bf16[2,128,4096]{2,1,0:T(8,128)(2,1)} %pad_maximum_fusion.2), calls=%async_computation.2 | async-start | bytes 4194304 | tf_op jit(solution)/shard_map/all_to_all | solution.py:65
  192.1 1.5 pad_maximum_fusion.5
  193.6 6.7 %concatenate.23 = f32[128,9218]{1,0:T(8,128)} concatenate(f32[128,257]{1,0:T(8,128)S(1)} %broadcast.29, f32[128,256]{1,0:T(8,128)S(1)} %collective-permute-done.10, f32[128,8192]{1,0:T(8,128)} %copy-done.5, f32[128,513]{1,0:T(8,128)S(1)} %broadcast.30), dimensions={1} | concatenate | bytes 9439232 | tf_op jit(solution)/shard_map/concatenate | solution.py:35
  200.3 1.8 dynamic_update_slice.23
  202.2 13.2 %all-to-all-done.2 = bf16[2,128,4096]{2,1,0:T(8,128)(2,1)} async-done(((bf16[2,128,4096]{2,1,0:T(8,128)(2,1)}), bf16[2,128,4096]{2,1,0:T(8,128)(2,1)}, u32[]{:S(2)}, u32[]{:S(2)}) %all-to-all-start.2) | async-done | bytes 2097184 | tf_op jit(solution)/shard_map/all_to_all | solution.py:65
  215.4 3.8 %all-to-all-start.3 = ((bf16[2,128,4096]{2,1,0:T(8,128)(2,1)}), bf16[2,128,4096]{2,1,0:T(8,128)(2,1)S(1)}, u32[]{:S(2)}, u32[]{:S(2)}) async-start(bf16[2,128,4096]{2,1,0:T(8,128)(2,1)} %pad_maximum_fusion.3), calls=%async_computation.3 | async-start | bytes 4194304 | tf_op jit(solution)/shard_map/all_to_all | solution.py:65
  219.1 18.9 %fusion.7 = bf16[128,8192]{1,0:T(8,128)(2,1)} fusion(f32[128,8192]{1,0:T(8,128)} %copy-done.1, f32[128,9218]{1,0:T(8,128)} %dynamic_update_slice.23, pred[8192]{0:T(1024)(128)(4,1)S(1)} %get-tuple-element.6, pred[8192]{0:T(1024)(128)(4,1)S(1)} %get-tuple-element.7, pred[8192]{0:T(1024)(128)(4,1)S(1)} %get-tuple-element.8, ...), kind=kLoop, calls=%fused_computation.14 | loop fusion | flops 18874368 | bytes 44105728 | tf_op jit(solution)/shard_map/convert_element_type | solution.py:60
  238.0 5.5 %all-to-all-done.3 = bf16[2,128,4096]{2,1,0:T(8,128)(2,1)S(1)} async-done(((bf16[2,128,4096]{2,1,0:T(8,128)(2,1)}), bf16[2,128,4096]{2,1,0:T(8,128)(2,1)S(1)}, u32[]{:S(2)}, u32[]{:S(2)}) %all-to-all-start.3) | async-done | bytes 2097184 | tf_op jit(solution)/shard_map/all_to_all | solution.py:65
  243.5 4.8 %all-to-all-start.4 = ((bf16[2,128,4096]{2,1,0:T(8,128)(2,1)}), bf16[2,128,4096]{2,1,0:T(8,128)(2,1)}, u32[]{:S(2)}, u32[]{:S(2)}) async-start(bf16[2,128,4096]{2,1,0:T(8,128)(2,1)} %pad_maximum_fusion.4), calls=%async_computation.4 | async-start | bytes 4194304 | tf_op jit(solution)/shard_map/all_to_all | solution.py:65
  248.3 1.7 slice_bitcast_fusion.1
  250.0 1.5 pad_maximum_fusion.6
  251.6 22.5 %all-to-all-done.4 = bf16[2,128,4096]{2,1,0:T(8,128)(2,1)} async-done(((bf16[2,128,4096]{2,1,0:T(8,128)(2,1)}), bf16[2,128,4096]{2,1,0:T(8,128)(2,1)}, u32[]{:S(2)}, u32[]{:S(2)}) %all-to-all-start.4) | async-done | bytes 2097184 | tf_op jit(solution)/shard_map/all_to_all | solution.py:65
  274.0 4.8 %all-to-all-start.5 = ((bf16[2,128,4096]{2,1,0:T(8,128)(2,1)}), bf16[2,128,4096]{2,1,0:T(8,128)(2,1)}, u32[]{:S(2)}, u32[]{:S(2)}) async-start(bf16[2,128,4096]{2,1,0:T(8,128)(2,1)} %pad_maximum_fusion.5), calls=%async_computation.5 | async-start | bytes 4194304 | tf_op jit(solution)/shard_map/all_to_all | solution.py:65
  278.9 2.4 fusion.64
  281.2 2.4 convolution_add_fusion.5
  283.7 4.4 %convolution_add_fusion.4 = f32[4096,256]{1,0:T(8,128)} fusion(f32[4096,256]{1,0:T(8,128)S(1)} %convolution_add_fusion.5, bf16[256,4096]{1,0:T(8,128)(2,1)} %bitcast.12, bf16[7,256,256]{2,1,0:T(8,128)(2,1)S(1)} %copy-done.7), kind=kOutput, calls=%fused_computation.6 | convolution fusion | flops 537919488 | bytes 10616832 | tf_op jit(solution)/shard_map/ip,io->po/dot_general | solution.py:70
  288.1 16.6 %all-to-all-done.5 = bf16[2,128,4096]{2,1,0:T(8,128)(2,1)} async-done(((bf16[2,128,4096]{2,1,0:T(8,128)(2,1)}), bf16[2,128,4096]{2,1,0:T(8,128)(2,1)}, u32[]{:S(2)}, u32[]{:S(2)}) %all-to-all-start.5) | async-done | bytes 2097184 | tf_op jit(solution)/shard_map/all_to_all | solution.py:65
  304.7 5.1 %all-to-all-start.6 = ((bf16[2,128,4096]{2,1,0:T(8,128)(2,1)}), bf16[2,128,4096]{2,1,0:T(8,128)(2,1)}, u32[]{:S(2)}, u32[]{:S(2)}) async-start(bf16[2,128,4096]{2,1,0:T(8,128)(2,1)} %pad_maximum_fusion.6), calls=%async_computation.6 | async-start | bytes 4194304 | tf_op jit(solution)/shard_map/all_to_all | solution.py:65
  309.8 3.0 convolution_add_fusion.3
  312.8 2.4 convolution_add_fusion.2
  315.2 4.4 %convolution_add_fusion.1 = f32[4096,256]{1,0:T(8,128)} fusion(f32[4096,256]{1,0:T(8,128)S(1)} %convolution_add_fusion.2, bf16[256,4096]{1,0:T(8,128)(2,1)} %bitcast.24, bf16[7,256,256]{2,1,0:T(8,128)(2,1)S(1)} %copy-done.7), kind=kOutput, calls=%fused_computation.3 | convolution fusion | flops 537919488 | bytes 10616832 | tf_op jit(solution)/shard_map/ip,io->po/dot_general | solution.py:70
  319.6 14.9 %all-to-all-done.6 = bf16[2,128,4096]{2,1,0:T(8,128)(2,1)} async-done(((bf16[2,128,4096]{2,1,0:T(8,128)(2,1)}), bf16[2,128,4096]{2,1,0:T(8,128)(2,1)}, u32[]{:S(2)}, u32[]{:S(2)}) %all-to-all-start.6) | async-done | bytes 2097184 | tf_op jit(solution)/shard_map/all_to_all | solution.py:65
  334.6 4.5 %fusion.3 = bf16[1,4096,256]{2,1,0:T(8,128)(2,1)} fusion(f32[4096,256]{1,0:T(8,128)} %convolution_add_fusion.1, bf16[256,4096]{1,0:T(8,128)(2,1)} %bitcast.28, f32[256]{0:T(256)S(1)} %copy-done.9, pred[4096]{0:T(1024)(128)(4,1)S(1)} %add_compare_fusion, bf16[7,256,256]{2,1,0:T(8,128)(2,1)S(1)} %copy-done.7), kind=kOutput, calls=%fused_computation.9 | convolution fusion | flops 541065216 | bytes 8524800 | tf_op jit(solution)/shard_map/ip,io->po/dot_general | solution.py:70
  (47 shorter events, 0.6 us)
Async XLA Ops:
  1.7 6.3 %copy-start.4 = (bf16[128,8192]{1,0:T(8,128)(2,1)S(1)}, bf16[128,8192]{1,0:T(8,128)(2,1)}, u32[]{:S(2)}) copy-start(bf16[128,8192]{1,0:T(8,128)(2,1)} %param.5) | copy-start | bytes 6291460
  3.2 153.7 %all-to-all-start = ((bf16[2,128,4096]{2,1,0:T(8,128)(2,1)}), bf16[2,128,4096]{2,1,0:T(8,128)(2,1)}, u32[]{:S(2)}, u32[]{:S(2)}) async-start(bf16[2,128,4096]{2,1,0:T(8,128)(2,1)} %pad_maximum_fusion), calls=%async_computation | async-start | bytes 4194304 | tf_op jit(solution)/shard_map/all_to_all | solution.py:65
  8.0 5.8 %copy-start.8 = (s32[8,8192]{1,0:T(8,128)S(1)}, s32[8,8192]{1,0:T(8,128)}, u32[]{:S(2)}) copy-start(s32[8,8192]{1,0:T(8,128)} %param.6) | copy-start | bytes 786436
  12.0 4.4 %collective-permute-start = (f32[128,256]{1,0:T(8,128)S(1)}, f32[128,256]{1,0:T(8,128)S(1)}, u32[]{:S(2)}, u32[]{:S(2)}) collective-permute-start(f32[128,256]{1,0:T(8,128)S(1)} %constant_dynamic-slice_fusion.5), channel_id=1, source_target_pairs={{0,1},{1,4},{4,5},{5,8},{8,9},{9,12},{12,13},{13,0},{2,3},{3,6},{6... | collective-permute-start | bytes 393224 | tf_op jit(solution)/shard_map/ppermute | solution.py:14
  12.1 8.7 %collective-permute-start.1 = (f32[128,256]{1,0:T(8,128)S(1)}, f32[128,256]{1,0:T(8,128)S(1)}, u32[]{:S(2)}, u32[]{:S(2)}) collective-permute-start(f32[128,256]{1,0:T(8,128)S(1)} %slice.341), channel_id=1, source_target_pairs={{0,13},{1,0},{4,1},{5,4},{8,5},{9,8},{12,9},{13,12},{2,15},{3,2},{... | collective-permute-start | bytes 393224 | tf_op jit(solution)/shard_map/ppermute | solution.py:14
  39.3 3.5 %copy-start.3 = (f32[128,8192]{1,0:T(8,128)}, f32[128,8192]{1,0:T(8,128)S(1)}, u32[]{:S(2)}) copy-start(f32[128,8192]{1,0:T(8,128)S(1)} %get-tuple-element.22) | copy-start | bytes 12582916
  39.6 4.4 %collective-permute-start.2 = (f32[128,256]{1,0:T(8,128)S(1)}, f32[128,256]{1,0:T(8,128)S(1)}, u32[]{:S(2)}, u32[]{:S(2)}) collective-permute-start(f32[128,256]{1,0:T(8,128)S(1)} %get-tuple-element.32), channel_id=1, source_target_pairs={{0,1},{1,4},{4,5},{5,8},{8,9},{9,12},{12,13},{13,0},{2,3},{3,6},{6... | collective-permute-start | bytes 393224 | tf_op jit(solution)/shard_map/ppermute | solution.py:14
  39.7 11.1 %collective-permute-start.3 = (f32[128,256]{1,0:T(8,128)S(1)}, f32[128,256]{1,0:T(8,128)S(1)}, u32[]{:S(2)}, u32[]{:S(2)}) collective-permute-start(f32[128,256]{1,0:T(8,128)S(1)} %get-tuple-element.31), channel_id=1, source_target_pairs={{0,13},{1,0},{4,1},{5,4},{8,5},{9,8},{12,9},{13,12},{2,15},{3,2},{... | collective-permute-start | bytes 393224 | tf_op jit(solution)/shard_map/ppermute | solution.py:14
  70.3 6.5 %copy-start.2 = (f32[128,8192]{1,0:T(8,128)}, f32[128,8192]{1,0:T(8,128)S(1)}, u32[]{:S(2)}) copy-start(f32[128,8192]{1,0:T(8,128)S(1)} %get-tuple-element.20) | copy-start | bytes 12582916
  73.6 4.4 %collective-permute-start.4 = (f32[128,256]{1,0:T(8,128)S(1)}, f32[128,256]{1,0:T(8,128)S(1)}, u32[]{:S(2)}, u32[]{:S(2)}) collective-permute-start(f32[128,256]{1,0:T(8,128)S(1)} %get-tuple-element.30), channel_id=1, source_target_pairs={{0,1},{1,4},{4,5},{5,8},{8,9},{9,12},{12,13},{13,0},{2,3},{3,6},{6... | collective-permute-start | bytes 393224 | tf_op jit(solution)/shard_map/ppermute | solution.py:14
  74.6 10.2 %collective-permute-start.5 = (f32[128,256]{1,0:T(8,128)S(1)}, f32[128,256]{1,0:T(8,128)S(1)}, u32[]{:S(2)}, u32[]{:S(2)}) collective-permute-start(f32[128,256]{1,0:T(8,128)S(1)} %get-tuple-element.29), channel_id=1, source_target_pairs={{0,13},{1,0},{4,1},{5,4},{8,5},{9,8},{12,9},{13,12},{2,15},{3,2},{... | collective-permute-start | bytes 393224 | tf_op jit(solution)/shard_map/ppermute | solution.py:14
  105.3 7.6 %copy-start = (f32[128,8192]{1,0:T(8,128)}, f32[128,8192]{1,0:T(8,128)S(1)}, u32[]{:S(2)}) copy-start(f32[128,8192]{1,0:T(8,128)S(1)} %get-tuple-element.18) | copy-start | bytes 12582916
  108.6 4.4 %collective-permute-start.6 = (f32[128,256]{1,0:T(8,128)S(1)}, f32[128,256]{1,0:T(8,128)S(1)}, u32[]{:S(2)}, u32[]{:S(2)}) collective-permute-start(f32[128,256]{1,0:T(8,128)S(1)} %get-tuple-element.28), channel_id=1, source_target_pairs={{0,1},{1,4},{4,5},{5,8},{8,9},{9,12},{12,13},{13,0},{2,3},{3,6},{6... | collective-permute-start | bytes 393224 | tf_op jit(solution)/shard_map/ppermute | solution.py:14
  111.4 8.4 %collective-permute-start.7 = (f32[128,256]{1,0:T(8,128)S(1)}, f32[128,256]{1,0:T(8,128)S(1)}, u32[]{:S(2)}, u32[]{:S(2)}) collective-permute-start(f32[128,256]{1,0:T(8,128)S(1)} %get-tuple-element.27), channel_id=1, source_target_pairs={{0,13},{1,0},{4,1},{5,4},{8,5},{9,8},{12,9},{13,12},{2,15},{3,2},{... | collective-permute-start | bytes 393224 | tf_op jit(solution)/shard_map/ppermute | solution.py:14
  140.5 7.9 %copy-start.1 = (f32[128,8192]{1,0:T(8,128)}, f32[128,8192]{1,0:T(8,128)S(1)}, u32[]{:S(2)}) copy-start(f32[128,8192]{1,0:T(8,128)S(1)} %get-tuple-element.16) | copy-start | bytes 12582916
  140.5 7.8 %collective-permute-start.8 = (f32[128,256]{1,0:T(8,128)S(1)}, f32[128,256]{1,0:T(8,128)S(1)}, u32[]{:S(2)}, u32[]{:S(2)}) collective-permute-start(f32[128,256]{1,0:T(8,128)S(1)} %get-tuple-element.26), channel_id=1, source_target_pairs={{0,1},{1,4},{4,5},{5,8},{8,9},{9,12},{12,13},{13,0},{2,3},{3,6},{6... | collective-permute-start | bytes 393224 | tf_op jit(solution)/shard_map/ppermute | solution.py:14
  145.1 10.0 %collective-permute-start.9 = (f32[128,256]{1,0:T(8,128)S(1)}, f32[128,256]{1,0:T(8,128)S(1)}, u32[]{:S(2)}, u32[]{:S(2)}) collective-permute-start(f32[128,256]{1,0:T(8,128)S(1)} %get-tuple-element.25), channel_id=1, source_target_pairs={{0,13},{1,0},{4,1},{5,4},{8,5},{9,8},{12,9},{13,12},{2,15},{3,2},{... | collective-permute-start | bytes 393224 | tf_op jit(solution)/shard_map/ppermute | solution.py:14
  156.9 30.1 %all-to-all-start.1 = ((bf16[2,128,4096]{2,1,0:T(8,128)(2,1)}), bf16[2,128,4096]{2,1,0:T(8,128)(2,1)}, u32[]{:S(2)}, u32[]{:S(2)}) async-start(bf16[2,128,4096]{2,1,0:T(8,128)(2,1)} %pad_maximum_fusion.1), calls=%async_computation.1 | async-start | bytes 4194304 | tf_op jit(solution)/shard_map/all_to_all | solution.py:65
  180.7 2.1 copy-start.5
  182.8 9.1 %copy-start.6 = (bf16[128,8192]{1,0:T(8,128)(2,1)S(1)}, bf16[128,8192]{1,0:T(8,128)(2,1)}, u32[]{:S(2)}) copy-start(bf16[128,8192]{1,0:T(8,128)(2,1)} %get-tuple-element.13) | copy-start | bytes 6291460
  182.8 10.8 %collective-permute-start.10 = (f32[128,256]{1,0:T(8,128)S(1)}, f32[128,256]{1,0:T(8,128)S(1)}, u32[]{:S(2)}, u32[]{:S(2)}) collective-permute-start(f32[128,256]{1,0:T(8,128)S(1)} %get-tuple-element.24), channel_id=1, source_target_pairs={{0,1},{1,4},{4,5},{5,8},{8,9},{9,12},{12,13},{13,0},{2,3},{3,6},{6... | collective-permute-start | bytes 393224 | tf_op jit(solution)/shard_map/ppermute | solution.py:14
  187.1 13.2 %collective-permute-start.11 = (f32[128,256]{1,0:T(8,128)S(1)}, f32[128,256]{1,0:T(8,128)S(1)}, u32[]{:S(2)}, u32[]{:S(2)}) collective-permute-start(f32[128,256]{1,0:T(8,128)S(1)} %get-tuple-element.23), channel_id=1, source_target_pairs={{0,13},{1,0},{4,1},{5,4},{8,5},{9,8},{12,9},{13,12},{2,15},{3,2},{... | collective-permute-start | bytes 393224 | tf_op jit(solution)/shard_map/ppermute | solution.py:14
  187.1 28.3 %all-to-all-start.2 = ((bf16[2,128,4096]{2,1,0:T(8,128)(2,1)}), bf16[2,128,4096]{2,1,0:T(8,128)(2,1)}, u32[]{:S(2)}, u32[]{:S(2)}) async-start(bf16[2,128,4096]{2,1,0:T(8,128)(2,1)} %pad_maximum_fusion.2), calls=%async_computation.2 | async-start | bytes 4194304 | tf_op jit(solution)/shard_map/all_to_all | solution.py:65
  215.4 28.2 %all-to-all-start.3 = ((bf16[2,128,4096]{2,1,0:T(8,128)(2,1)}), bf16[2,128,4096]{2,1,0:T(8,128)(2,1)S(1)}, u32[]{:S(2)}, u32[]{:S(2)}) async-start(bf16[2,128,4096]{2,1,0:T(8,128)(2,1)} %pad_maximum_fusion.3), calls=%async_computation.3 | async-start | bytes 4194304 | tf_op jit(solution)/shard_map/all_to_all | solution.py:65
  243.5 30.5 %all-to-all-start.4 = ((bf16[2,128,4096]{2,1,0:T(8,128)(2,1)}), bf16[2,128,4096]{2,1,0:T(8,128)(2,1)}, u32[]{:S(2)}, u32[]{:S(2)}) async-start(bf16[2,128,4096]{2,1,0:T(8,128)(2,1)} %pad_maximum_fusion.4), calls=%async_computation.4 | async-start | bytes 4194304 | tf_op jit(solution)/shard_map/all_to_all | solution.py:65
  250.0 28.9 %copy-start.7 = (bf16[7,256,256]{2,1,0:T(8,128)(2,1)S(1)}, bf16[7,256,256]{2,1,0:T(8,128)(2,1)}, u32[]{:S(2)}) copy-start(bf16[7,256,256]{2,1,0:T(8,128)(2,1)} %param.8) | copy-start | bytes 2752516
  274.0 30.7 %all-to-all-start.5 = ((bf16[2,128,4096]{2,1,0:T(8,128)(2,1)}), bf16[2,128,4096]{2,1,0:T(8,128)(2,1)}, u32[]{:S(2)}, u32[]{:S(2)}) async-start(bf16[2,128,4096]{2,1,0:T(8,128)(2,1)} %pad_maximum_fusion.5), calls=%async_computation.5 | async-start | bytes 4194304 | tf_op jit(solution)/shard_map/all_to_all | solution.py:65
  304.7 29.9 %all-to-all-start.6 = ((bf16[2,128,4096]{2,1,0:T(8,128)(2,1)}), bf16[2,128,4096]{2,1,0:T(8,128)(2,1)}, u32[]{:S(2)}, u32[]{:S(2)}) async-start(bf16[2,128,4096]{2,1,0:T(8,128)(2,1)} %pad_maximum_fusion.6), calls=%async_computation.6 | async-start | bytes 4194304 | tf_op jit(solution)/shard_map/all_to_all | solution.py:65
  315.2 19.4 %copy-start.9 = (f32[256]{0:T(256)S(1)}, f32[256]{0:T(256)}, u32[]{:S(2)}) copy-start(f32[256]{0:T(256)} %param.9) | copy-start | bytes 3076
